TPU v7x, 32 devices: a whole 2x2x4 slice. The times are simulated.
32 devices in a mesh: col: 4 (over y, core), row: 8 (over z, x).
Axes of the slice: x: 2, y: 2, z: 4, core: 2. Of those that a mesh axis runs over, the one named last changes fastest.
Arguments:
- pair_rep: float32 [32, 32, 128], P('row', 'col'), may hold values from -6 to 6
- cotangent: float32 [32, 32, 128], P('row', 'col'), may hold values from -6 to 6
- chain_ids: int32 [32], replicated, may hold values from 0 to 3, never falling along the last dimension, each value on 1 to 16 neighbouring positions
- template: int32 [8, 8], replicated, may hold values from 0 to 1
- norm_gain: float32 [128], replicated, may hold values from 0.25 to 1.75
- w_query: float32 [128, 128], replicated
- w_key: float32 [128, 128], replicated
- w_value: float32 [128, 128], replicated, may hold values from -0.5 to 0.5
- w_gate: float32 [128, 128], replicated, may hold values from -0.5 to 0.5
- gate_bias: float32 [128], replicated, may hold values from -4 to 4
- w_out: float32 [128, 128], replicated, may hold values from -0.5 to 0.5
- w_bias: float32 [4, 128], replicated, may hold values from -0.5 to 0.5
Outputs:
- update: float32 [32, 32, 128], P('row', 'col')
- grad_pair: float32 [32, 32, 128], P('row', 'col')
- grad_query: float32 [128, 128], replicated
- grad_key: float32 [128, 128], replicated
- grad_value: float32 [128, 128], replicated
- grad_gate: float32 [128, 128], replicated
- grad_gate_bias: float32 [128], replicated
- grad_out: float32 [128, 128], replicated
- grad_bias: float32 [4, 128], replicated
- grad_gain: float32 [128], replicated
All inputs are finite; a program needn't handle non-finite values.
Results may differ from a plain program's by a relative error of at most 0.0003.
Values sent between devices are 32-bit elements; how exact they have to be, the bound alone decides.
A program may use at most 64 MiB of HBM per device.

v0:
```python
import jax
import jax.numpy as jnp
from jax import lax
from jax.sharding import PartitionSpec as P

HIGHEST = lax.Precision.HIGHEST
NEG_FILL = -1000000000.0


def matmul(left, right):
    return jnp.dot(left, right, precision=HIGHEST, preferred_element_type=jnp.float32)


def attend_dense(queries, keys_col, values_col, bias_rows, keep_col, factor):
    scores = jnp.einsum("ihd,khd->ihk", queries, keys_col, precision=HIGHEST) * factor + bias_rows
    scores = jnp.where(keep_col[None, None, :], scores, NEG_FILL)
    highest = jnp.max(scores, axis=2, keepdims=True)
    weights = jnp.exp(scores - highest)
    normed_weights = weights / jnp.sum(weights, axis=2, keepdims=True)
    output = jnp.einsum("ihk,khd->ihd", normed_weights, values_col, precision=HIGHEST)
    return (output, normed_weights)


def attend_dense_back(queries, keys_col, values_col, normed_weights, output, d_output, factor):
    d_weights = jnp.einsum("ihd,khd->ihk", d_output, values_col, precision=HIGHEST)
    centred = jnp.sum(d_output * output, axis=2, keepdims=True)
    d_scores = normed_weights * (d_weights - centred)
    d_query = jnp.einsum("ihk,khd->ihd", d_scores, keys_col, precision=HIGHEST) * factor
    d_key = jnp.einsum("ihk,ihd->khd", d_scores, queries, precision=HIGHEST) * factor
    d_value = jnp.einsum("ihk,ihd->khd", normed_weights, d_output, precision=HIGHEST)
    return (d_query, d_key, d_value, d_scores)


def body(
    pair_rep,
    cotangent,
    chain_ids,
    template,
    norm_gain,
    w_query,
    w_key,
    w_value,
    w_gate,
    gate_bias,
    w_out,
    w_bias,
):
    column_cells, upstream = (
        lax.all_to_all(pair_rep, "row", split_axis=1, concat_axis=0, tiled=True),
        lax.all_to_all(cotangent, "row", split_axis=1, concat_axis=0, tiled=True),
    )
    tokens, cols, width = column_cells.shape
    head_count = w_bias.shape[0]
    head_depth = width // head_count
    factor = head_depth ** (-0.5)
    row_count = lax.axis_size("row")
    linear = lax.axis_index("col") * row_count + lax.axis_index("row")
    first_col = linear * cols
    own_chain = lax.dynamic_slice_in_dim(chain_ids, first_col, cols, 0)
    same_chain = chain_ids[:, None] == own_chain[None, :]
    block_count = template.shape[0]
    block_width = tokens // block_count
    own_block = (first_col + jnp.arange(cols, dtype=jnp.int32)) // block_width
    picker = (jnp.arange(block_count, dtype=jnp.int32)[:, None] == own_block[None, :]).astype(
        jnp.int32
    )
    block_keep = jnp.sum(template[:, :, None] * picker[None, :, :], axis=1)
    keep_mask = same_chain | (jnp.repeat(block_keep, block_width, axis=0) > 0)
    cells = column_cells.reshape(tokens * cols, width)
    center = jnp.mean(cells, axis=-1, keepdims=True)
    shifted = cells - center
    spread = jnp.mean(shifted * shifted, axis=-1, keepdims=True)
    inverse = lax.rsqrt(spread + 1e-05)
    scaled = shifted * inverse
    normed = scaled * norm_gain
    queries = matmul(normed, w_query).reshape(tokens, cols, head_count, head_depth)
    keys_all = matmul(normed, w_key).reshape(tokens, cols, head_count, head_depth)
    values_all = matmul(normed, w_value).reshape(tokens, cols, head_count, head_depth)
    gate = jax.nn.sigmoid(matmul(normed, w_gate) + gate_bias)
    normed_cols = normed.reshape(tokens, cols, width)
    bias_piece = jnp.einsum("ktc,hc->thk", normed_cols, w_bias, precision=HIGHEST)
    bias_rows = lax.all_gather(bias_piece, ("col", "row"), axis=0, tiled=True)
    actives = []
    slot = 0
    keep_col = keep_mask[:, slot]
    active = jnp.any(keep_col.reshape(block_count, block_width), axis=1)
    actives.append(active)
    attended_slot, kept_stat = attend_dense(
        queries[:, slot], keys_all[:, slot], values_all[:, slot], bias_rows, keep_col, factor
    )
    outputs = [attended_slot]
    saved = [kept_stat]
    attended = jnp.stack(outputs, axis=1).reshape(tokens * cols, width)
    gated = gate * attended
    update_cols = matmul(gated, w_out).reshape(tokens, cols, width)
    update_block = lax.all_to_all(update_cols, "row", split_axis=0, concat_axis=1, tiled=True)
    d_cells = upstream.reshape(tokens * cols, width)
    d_gated = matmul(d_cells, jnp.transpose(w_out))
    grad_out_w = matmul(jnp.transpose(gated), d_cells)
    d_attended = (d_gated * gate).reshape(tokens, cols, head_count, head_depth)
    d_gate_pre = d_gated * attended * gate * (1.0 - gate)
    slot = 0
    query_grad, key_grad, value_grad, score_grad = attend_dense_back(
        queries[:, slot],
        keys_all[:, slot],
        values_all[:, slot],
        saved[slot],
        outputs[slot],
        d_attended[:, slot],
        factor,
    )
    d_queries = [query_grad]
    d_keys = [key_grad]
    d_values = [value_grad]
    d_query = jnp.stack(d_queries, axis=1).reshape(tokens * cols, width)
    d_key = jnp.stack(d_keys, axis=1).reshape(tokens * cols, width)
    d_value = jnp.stack(d_values, axis=1).reshape(tokens * cols, width)
    bias_grad = lax.psum_scatter(score_grad, ("col", "row"), scatter_dimension=0, tiled=True)
    bias_back = jnp.einsum("thk,hc->ktc", bias_grad, w_bias, precision=HIGHEST).reshape(
        tokens * cols, width
    )
    grad_bias_w = jnp.einsum("thk,ktc->hc", bias_grad, normed_cols, precision=HIGHEST)
    d_normed = (
        matmul(d_query, jnp.transpose(w_query))
        + matmul(d_key, jnp.transpose(w_key))
        + matmul(d_value, jnp.transpose(w_value))
        + matmul(d_gate_pre, jnp.transpose(w_gate))
        + bias_back
    )
    grad_query_w = matmul(jnp.transpose(normed), d_query)
    grad_key_w = matmul(jnp.transpose(normed), d_key)
    grad_value_w = matmul(jnp.transpose(normed), d_value)
    grad_gate_w = matmul(jnp.transpose(normed), d_gate_pre)
    grad_gate_shift = jnp.sum(d_gate_pre, axis=0)
    grad_gain_w = jnp.sum(d_normed * scaled, axis=0)
    d_scaled = d_normed * norm_gain
    mean_term = jnp.mean(d_scaled, axis=-1, keepdims=True)
    cross_term = jnp.mean(d_scaled * scaled, axis=-1, keepdims=True)
    d_input = inverse * (d_scaled - mean_term - scaled * cross_term)
    grad_block = lax.all_to_all(
        d_input.reshape(tokens, cols, width), "row", split_axis=0, concat_axis=1, tiled=True
    )
    summed = lax.psum(
        (
            grad_query_w,
            grad_key_w,
            grad_value_w,
            grad_gate_w,
            grad_gate_shift,
            grad_out_w,
            grad_bias_w,
            grad_gain_w,
        ),
        ("col", "row"),
    )
    return (
        update_block,
        grad_block,
        summed[0] / tokens,
        summed[1] / tokens,
        summed[2] / tokens,
        summed[3] / tokens,
        summed[4] / tokens,
        summed[5] / tokens,
        summed[6] / tokens,
        summed[7] / tokens,
    )


def solution(mesh):
    in_specs = (
        P("row", "col", None),
        P("row", "col", None),
        P(),
        P(),
        P(),
        P(),
        P(),
        P(),
        P(),
        P(),
        P(),
        P(),
    )
    out_specs = (
        P("row", "col", None),
        P("row", "col", None),
        P(),
        P(),
        P(),
        P(),
        P(),
        P(),
        P(),
        P(),
    )
    return jax.shard_map(body, mesh=mesh, in_specs=in_specs, out_specs=out_specs, check_vma=False)
```

profile of v0, /device:TPU:0, one launch (start us, length us, event | category | flops | bytes accessed | tf_op | source)
XLA Modules:
  0.0 330.8 jit_solution(3172362263427909319)
XLA Ops:
  7.2 1.4 copy.65
  8.6 7.4 %all-to-all-start = ((f32[4,8,128]{2,0,1:T(4,128)}), f32[4,8,128]{2,0,1:T(4,128)S(1)}, u32[]{:S(2)}, u32[]{:S(2)}) async-start(f32[4,8,128]{2,0,1:T(4,128)} %copy.65), calls=%async_computation | async-start | bytes 32768 | tf_op jit(solution)/shard_map/all_to_all | solution.py:49
  16.0 0.6 copy-done.11
  16.9 0.6 dynamic_slice.3
  17.5 0.7 compare_or_fusion
  18.2 0.6 copy.81
  18.9 0.7 copy-done.3
  19.7 0.7 copy-done.4
  20.6 1.9 all-to-all-done
  22.5 4.1 %all-to-all-start.2 = ((f32[4,8,128]{2,0,1:T(4,128)}), f32[4,8,128]{2,0,1:T(4,128)S(1)}, u32[]{:S(2)}, u32[]{:S(2)}) async-start(f32[4,8,128]{2,0,1:T(4,128)} %copy.81), calls=%async_computation.2 | async-start | bytes 32768 | tf_op jit(solution)/shard_map/all_to_all | solution.py:50
  27.0 0.6 copy-done.14
  27.9 67.6 %all-gather.1 = f32[32,4,32]{2,1,0:T(4,128)S(1)} all-gather(f32[1,4,32]{2,1,0:T(4,128)S(1)} %convolution_bitcast_fusion.1), channel_id=2, replica_groups=mesh['col'=4,'row'=8] {'col','row'}, dimensions={0}, use_global_device_ids=true | all-gather | bytes 16896 | tf_op jit(solution)/shard_map/all_gather | solution.py:82
  97.6 0.8 copy-done.1
  99.3 0.8 fusion.29
  100.0 0.9 fusion.27
  102.2 3.3 %all-to-all-start.1 = ((f32[32,1,128]{2,1,0:T(1,128)}), f32[32,1,128]{2,1,0:T(1,128)S(1)}, u32[]{:S(2)}, u32[]{:S(2)}) async-start(f32[32,1,128]{2,1,0:T(1,128)} %bitcast.22), calls=%async_computation.1 | async-start | bytes 32768 | tf_op jit(solution)/shard_map/all_to_all | solution.py:96
  105.6 40.0 %all-reduce = f32[32,4,32]{2,1,0:T(4,128)S(1)} all-reduce(f32[32,4,32]{2,1,0:T(4,128)S(1)} %copy.90), channel_id=3, replica_groups=mesh['col'=4,'row'=8] {'col','row'}, use_global_device_ids=true, to_apply=%region_6.7.clone | all-reduce | flops 4096 | bytes 32768
  145.8 1.0 fusion.44
  146.8 0.9 fusion.45
  147.9 0.9 fusion.46
  149.1 1.0 fusion.17
  150.9 41.0 %all-reduce.1 = (f32[128]{0:T(128)S(1)}, f32[4,128]{1,0:T(4,128)S(1)}, f32[128]{0:T(128)S(1)}) all-reduce(f32[128]{0:T(128)S(1)} %get-tuple-element.21, f32[4,128]{1,0:T(4,128)S(1)} %fusion.12, f32[128]{0:T(128)S(1)} %get-tuple-element.10), channel_id=1, replica_groups=mesh['col'=4,'row'=8] {'col','row'}, use_global_device_ids=true, to_apply=%region_14.15 | all-reduce | flops 768 | bytes 6144 | tf_op jit(solution)/shard_map/psum | solution.py:143
  191.9 0.7 subtract_multiply_fusion
  192.6 0.6 broadcast_multiply_fusion.6
  193.2 5.3 %all-to-all-start.3 = ((f32[32,1,128]{2,1,0:T(1,128)}), f32[32,1,128]{2,1,0:T(1,128)S(1)}, u32[]{:S(2)}, u32[]{:S(2)}) async-start(f32[32,1,128]{2,1,0:T(1,128)} %bitcast.39), calls=%async_computation.3 | async-start | bytes 32768 | tf_op jit(solution)/shard_map/all_to_all | solution.py:140
  199.1 0.6 copy.109
  199.7 5.5 %all-to-all-done.3 = f32[32,1,128]{2,1,0:T(1,128)S(1)} async-done(((f32[32,1,128]{2,1,0:T(1,128)}), f32[32,1,128]{2,1,0:T(1,128)S(1)}, u32[]{:S(2)}, u32[]{:S(2)}) %all-to-all-start.3) | async-done | bytes 16416 | tf_op jit(solution)/shard_map/all_to_all | solution.py:140
  205.2 0.6 copy.108
  205.8 115.1 %all-reduce.5.cloned.1.call-done = (f32[128,128]{1,0:T(8,128)}, f32[128,128]{1,0:T(8,128)}, f32[128,128]{1,0:T(8,128)}, f32[128,128]{1,0:T(8,128)}, f32[128,128]{1,0:T(8,128)}) async-done(((f32[128,128]{1,0:T(8,128)}, f32[128,128]{1,0:T(8,128)}, f32[128,128]{1,0:T(8,128)}, f32[128,128]{1,0:T(8,128)}, f32[128,128]{1,0:T(8,128)}), (f32[128,128]{1,0:T(8,128)}, f32[128,128]{1,0:T(8,128)}, f32[128,128]{1,0:T(8,128)}, ...) | async-done | bytes 327696 | tf_op jit(solution)/shard_map/psum | solution.py:143
  320.8 1.5 broadcast_multiply_fusion.4
  322.4 0.7 broadcast_multiply_fusion.2
  323.3 0.7 broadcast_multiply_fusion
  (70 shorter events, 7.7 us)
Async XLA Ops:
  7.2 91.4 %copy-start = (f32[128,128]{1,0:T(8,128)S(1)}, f32[128,128]{1,0:T(8,128)}, u32[]{:S(2)}) copy-start(f32[128,128]{1,0:T(8,128)} %param.20) | copy-start | bytes 196612
  8.5 10.2 %copy-start.2 = (f32[128,128]{1,0:T(8,128)S(1)}, f32[128,128]{1,0:T(8,128)}, u32[]{:S(2)}) copy-start(f32[128,128]{1,0:T(8,128)} %param.17) | copy-start | bytes 196612
  8.6 14.0 %all-to-all-start = ((f32[4,8,128]{2,0,1:T(4,128)}), f32[4,8,128]{2,0,1:T(4,128)S(1)}, u32[]{:S(2)}, u32[]{:S(2)}) async-start(f32[4,8,128]{2,0,1:T(4,128)} %copy.65), calls=%async_computation | async-start | bytes 32768 | tf_op jit(solution)/shard_map/all_to_all | solution.py:49
  15.9 0.7 copy-start.11
  15.9 1.0 copy-start.13
  16.0 2.2 copy-start.9
  18.8 0.8 copy-start.3
  19.6 0.8 copy-start.4
  22.5 75.1 %all-to-all-start.2 = ((f32[4,8,128]{2,0,1:T(4,128)}), f32[4,8,128]{2,0,1:T(4,128)S(1)}, u32[]{:S(2)}, u32[]{:S(2)}) async-start(f32[4,8,128]{2,0,1:T(4,128)} %copy.81), calls=%async_computation.2 | async-start | bytes 32768 | tf_op jit(solution)/shard_map/all_to_all | solution.py:50
  26.9 0.7 copy-start.14
  27.0 0.7 copy-start.10
  97.5 0.8 copy-start.1
  98.3 0.7 copy-start.12
  102.2 91.0 %all-to-all-start.1 = ((f32[32,1,128]{2,1,0:T(1,128)}), f32[32,1,128]{2,1,0:T(1,128)S(1)}, u32[]{:S(2)}, u32[]{:S(2)}) async-start(f32[32,1,128]{2,1,0:T(1,128)} %bitcast.22), calls=%async_computation.1 | async-start | bytes 32768 | tf_op jit(solution)/shard_map/all_to_all | solution.py:96
  105.6 215.3 %all-reduce.5.cloned.1.call-start = ((), (), s32[]{:S(2)}) async-start(), calls=%async_computation.4 | async-start | bytes 655360 | tf_op jit(solution)/shard_map/psum | solution.py:143
  193.2 11.9 %all-to-all-start.3 = ((f32[32,1,128]{2,1,0:T(1,128)}), f32[32,1,128]{2,1,0:T(1,128)S(1)}, u32[]{:S(2)}, u32[]{:S(2)}) async-start(f32[32,1,128]{2,1,0:T(1,128)} %bitcast.39), calls=%async_computation.3 | async-start | bytes 32768 | tf_op jit(solution)/shard_map/all_to_all | solution.py:140
  320.8 1.5 copy-start.7
  320.8 1.5 copy-start.8
  322.4 0.8 copy-start.5
  322.4 0.9 copy-start.6
Sparse Core Ops, SparseCore 0:
  193.4 127.4 all-reduce.4
where the time goes:
time: 332 us; the launch traced here: 331 us
  blocking collectives  149 us (45%)
  waiting for transfers between devices  122 us (37%)
  starting transfers between devices  20.2 us (6%)
  between operations  14.3 us (4%)
  matrix products  10.4 us (3%)
  local copies, waits for them, and re-layouts  8.98 us (3%)
  other arithmetic  5.79 us (2%)
    psum x1, waiting for transfers between devices, body(): lax.psum((grad_query_w, grad_key_w, grad_value_w, grad_gate_w, grad_gate_...  115 us
    all_gather x1, blocking collectives, body(): bias_rows = lax.all_gather(bias_piece, ('col', 'row'), axis=0, tiled=True)  67.6 us
    psum x1, blocking collectives, body(): lax.psum((grad_query_w, grad_key_w, grad_value_w, grad_gate_w, grad_gate_...  41 us
    unnamed x1, blocking collectives  40 us
    dot_general x15, matrix products, matmul(): jnp.dot(left, right, precision=HIGHEST, preferred_element_type=jnp.float32)  8.05 us
    all_to_all x1, starting transfers between devices, body(): lax.all_to_all(pair_rep, 'row', split_axis=1, concat_axis=0, tiled=True)  7.38 us
  transfers between devices with their start and end apart: 5, of which 3 were waited for; matrix products, arithmetic and copies ran while one was open for 4% of the time, Pallas kernels for 0%

commit v1 on v0

--- a/solution.py
+++ b/solution.py
@@ -1,6 +1,10 @@
+import functools
+
 import jax
 import jax.numpy as jnp
 from jax import lax
+from jax.experimental import pallas as pl
+from jax.experimental.pallas import tpu as pltpu
 from jax.sharding import PartitionSpec as P
 
 HIGHEST = lax.Precision.HIGHEST
@@ -31,7 +35,7 @@
     return (d_query, d_key, d_value, d_scores)
 
 
-def body(
+def body_collective(
     pair_rep,
     cotangent,
     chain_ids,
@@ -167,6 +171,375 @@
     )
 
 
+MESH = pl.DeviceIdType.MESH
+LANES = 128
+SUBLANES = 8
+MATRICES = 5
+CORE_SETS = ((0, 3), (3, 2))
+CELLS, BIAS, UPDATE, CELL_GRAD, SCORE_GRAD, SMALL, SCATTER, GATHER, FORWARD, PAIR = range(10)
+
+
+def dot(left, right, left_dim=1, right_dim=0):
+    return lax.dot_general(
+        left,
+        right,
+        (((left_dim,), (right_dim,)), ((), ())),
+        precision=HIGHEST,
+        preferred_element_type=jnp.float32,
+    )
+
+
+def layer_norm_parts(cells):
+    shifted = cells - jnp.mean(cells, axis=-1, keepdims=True)
+    inverse = lax.rsqrt(jnp.mean(shifted * shifted, axis=-1, keepdims=True) + 1e-05)
+    return shifted * inverse, inverse
+
+
+def layer_norm_back(d_scaled, scaled, inverse):
+    mean_term = jnp.mean(d_scaled, axis=-1, keepdims=True)
+    cross_term = jnp.mean(d_scaled * scaled, axis=-1, keepdims=True)
+    return inverse * (d_scaled - mean_term - scaled * cross_term)
+
+
+def fused_kernel(
+    row_count, col_count, tokens, heads, blocks,
+    pair_ref, cot_ref, chain_ref, template_ref, gain_ref,
+    wq_ref, wk_ref, wv_ref, wg_ref, gate_bias_ref, wo_ref, wb_ref,
+    update_out, pair_out, query_out, key_out, value_out, gate_out, gate_bias_out, wo_out, bias_out, gain_out,
+    cell_send, cell_recv, bias_send, bias_recv, bias_full, update_send, update_recv,
+    grad_send, grad_recv, score_send, score_recv, small_send, small_recv,
+    parts, pair_recv, scatter_recv, gather_send, final, send_sem, recv_sem,
+):
+    width = LANES
+    depth = width // heads
+    factor = depth ** (-0.5)
+    rows = tokens // row_count
+    cols = tokens // col_count
+    count = row_count * col_count
+    half_cols = col_count // 2
+    chips = count // 2
+    tile = width // chips
+    row = lax.axis_index("row")
+    col = lax.axis_index("col")
+    me = row * col_count + col
+    core = lax.rem(col, 2)
+    chip = row * half_cols + col // 2
+    partner = (col + 1 - 2 * core, row)
+
+    def device(index):
+        return (lax.rem(index, col_count), index // col_count)
+
+    def remote(src, dst, kind, target):
+        return pltpu.make_async_remote_copy(
+            src_ref=src, dst_ref=dst, send_sem=send_sem.at[kind], recv_sem=recv_sem.at[kind],
+            device_id=target, device_id_type=MESH,
+        )
+
+    def to_all(make):
+        def step(distance, carry):
+            make(lax.rem(me + distance, count)).start()
+            return carry
+        lax.fori_loop(1, count, step, 0)
+
+    def to_rows(make):
+        def step(distance, carry):
+            make(lax.rem(row + distance, row_count)).start()
+            return carry
+        lax.fori_loop(1, row_count, step, 0)
+
+    def wait_for(ref, sem, kind):
+        pltpu.make_async_copy(ref, ref, sem.at[kind]).wait()
+
+    barrier = pltpu.get_barrier_semaphore()
+
+    def greet(distance, carry):
+        pl.semaphore_signal(
+            barrier, inc=1, device_id=device(lax.rem(me + distance, count)), device_id_type=MESH
+        )
+        return carry
+
+    lax.fori_loop(1, count, greet, 0)
+
+    for slot in range(cols):
+        cell_send[slot, :rows, :] = pair_ref[:, slot, :]
+        cell_send[slot, rows:, :] = cot_ref[:, slot, :]
+    gain = gain_ref[...]
+    block_scaled, block_inverse = layer_norm_parts(pair_ref[...].reshape(rows * cols, width))
+    spread_bias = jnp.broadcast_to(wb_ref[...][:, None, :], (heads, tokens, width)).reshape(
+        heads * tokens, width
+    )
+    products = dot(block_scaled * gain, spread_bias, 1, 1).reshape(rows, cols, heads * tokens)
+    lane_token = lax.broadcasted_iota(jnp.int32, (1, cols, heads * tokens), 2) & (tokens - 1)
+    block_col = lax.broadcasted_iota(jnp.int32, (1, cols, heads * tokens), 1) + col * cols
+    own_lane = lane_token == block_col
+    bias_send[...] = jnp.sum(jnp.where(own_lane, products, 0.0), axis=1)
+    pl.semaphore_wait(barrier, count - 1)
+
+    to_rows(lambda r: remote(cell_send.at[r], cell_recv.at[row], CELLS, (col, r)))
+    to_all(lambda d: remote(bias_send, bias_recv.at[me], BIAS, device(d)))
+    cell_recv[row] = cell_send[row]
+    bias_recv[me] = bias_send[...]
+
+    own = col * cols + row
+    token_shift = (tokens // blocks).bit_length() - 1
+    chain_row = chain_ref[...].astype(jnp.float32)
+    square_row = lax.broadcasted_iota(jnp.int32, (tokens, tokens), 0)
+    square_col = lax.broadcasted_iota(jnp.int32, (tokens, tokens), 1)
+    chain_all = jnp.broadcast_to(chain_row, (tokens, tokens))
+    chain_col = jnp.sum(jnp.where(square_row == square_col, chain_all, 0.0), axis=1, keepdims=True)
+    own_chain = jnp.sum(jnp.where(square_col == own, chain_all, 0.0), axis=1, keepdims=True)
+    spread_row = (
+        lax.broadcasted_iota(jnp.int32, (tokens, blocks), 0) >> token_shift
+        == lax.broadcasted_iota(jnp.int32, (tokens, blocks), 1)
+    ).astype(jnp.float32)
+    spread_template = dot(spread_row, template_ref[...].astype(jnp.float32))
+    block_lane = lax.broadcasted_iota(jnp.int32, (tokens, blocks), 1)
+    template_col = jnp.sum(
+        jnp.where(block_lane == own >> token_shift, spread_template, 0.0), axis=1, keepdims=True
+    )
+    keep = (chain_col == own_chain) | (template_col > 0.5)
+    depth_shift = depth.bit_length() - 1
+    head_mask = (
+        lax.broadcasted_iota(jnp.int32, (heads, 1, width), 2) >> depth_shift
+        == lax.broadcasted_iota(jnp.int32, (heads, 1, width), 0)
+    ).astype(jnp.float32)
+
+    def by_head(array):
+        return (array[None] * head_mask).reshape(heads * tokens, width)
+
+    def own_head(array):
+        return jnp.sum(array.reshape(heads, tokens, width) * head_mask, axis=0)
+
+    wait_for(cell_recv.at[pl.ds(0, row_count - 1)], recv_sem, CELLS)
+    cells = jnp.concatenate([cell_recv[r, :rows, :] for r in range(row_count)], axis=0)
+    upstream = jnp.concatenate([cell_recv[r, rows:, :] for r in range(row_count)], axis=0)
+    scaled, inverse = layer_norm_parts(cells)
+    normed = scaled * gain
+    queries = dot(normed, wq_ref[...])
+    keys = dot(normed, wk_ref[...])
+    values = dot(normed, wv_ref[...])
+    gate = jax.nn.sigmoid(dot(normed, wg_ref[...]) + gate_bias_ref[...])
+    d_gated = dot(upstream, wo_ref[...], 1, 1)
+    d_attended_heads = by_head(d_gated * gate)
+    query_heads = by_head(queries)
+    scores = dot(keys, query_heads, 1, 1) * factor
+    d_weights = dot(values, d_attended_heads, 1, 1)
+
+    wait_for(bias_recv.at[pl.ds(0, count - 1)], recv_sem, BIAS)
+    bias_rows = jnp.sum(bias_recv[...].reshape(row_count, col_count, rows, heads * tokens), axis=1)
+    for r in range(row_count):
+        bias_full[r * rows : (r + 1) * rows, :] = bias_rows[r]
+    scores = jnp.where(keep, scores + bias_full[...], NEG_FILL)
+    weights = jnp.exp(scores - jnp.max(scores, axis=0, keepdims=True))
+    weights = weights / jnp.sum(weights, axis=0, keepdims=True)
+    d_scores = weights * (d_weights - jnp.sum(weights * d_weights, axis=0, keepdims=True))
+    for r in range(row_count):
+        score_send[r] = d_scores[r * rows : (r + 1) * rows, :]
+    to_all(lambda d: remote(score_send.at[d // col_count], score_recv.at[me], SCORE_GRAD, device(d)))
+    score_recv[me] = score_send[row]
+
+    def share(index, grad):
+        parts[index] = grad
+        owner = 0 if index < CORE_SETS[0][1] else 1
+
+        @pl.when(core != owner)
+        def _():
+            remote(parts.at[index], pair_recv.at[index], PAIR + index, partner).start()
+
+    attended = own_head(dot(weights, values, 0, 0))
+    gated = gate * attended
+    d_gate = d_gated * attended * gate * (1.0 - gate)
+    d_query = own_head(dot(d_scores, keys, 0, 0)) * factor
+    d_key = dot(d_scores, query_heads) * factor
+    d_value = dot(weights, d_attended_heads)
+    share(3, dot(normed, d_query, 0, 0))
+    share(4, dot(normed, d_key, 0, 0))
+    share(0, dot(gated, upstream, 0, 0))
+    share(1, dot(normed, d_gate, 0, 0))
+    share(2, dot(normed, d_value, 0, 0))
+
+    for which in range(2):
+        first, number = CORE_SETS[which]
+
+        @pl.when(core == which)
+        def _(first=first, number=number):
+            for index in range(first, first + number):
+                wait_for(pair_recv.at[index], recv_sem, PAIR + index)
+                parts[index] = parts[index] + pair_recv[index]
+
+            def step(distance, carry):
+                target = lax.rem(chip + distance, chips)
+                remote(
+                    parts.at[pl.ds(first, number), pl.ds(pl.multiple_of(target * tile, tile), tile), :],
+                    scatter_recv.at[chip, pl.ds(0, number)],
+                    SCATTER,
+                    (lax.rem(target, half_cols) * 2 + core, target // half_cols),
+                ).start()
+                return carry
+
+            lax.fori_loop(1, chips, step, 0)
+
+    d_normed = (
+        dot(d_query, wq_ref[...], 1, 1)
+        + dot(d_key, wk_ref[...], 1, 1)
+        + dot(d_value, wv_ref[...], 1, 1)
+        + dot(d_gate, wg_ref[...], 1, 1)
+    )
+    d_cells = layer_norm_back(d_normed * gain, scaled, inverse)
+    for r in range(row_count):
+        grad_send[r] = d_cells[r * rows : (r + 1) * rows, :]
+    to_rows(lambda r: remote(grad_send.at[r], grad_recv.at[row], CELL_GRAD, (col, r)))
+    grad_recv[row] = grad_send[row]
+    update = dot(gated, wo_ref[...])
+    for r in range(row_count):
+        update_send[r] = update[r * rows : (r + 1) * rows, :]
+    to_rows(lambda r: remote(update_send.at[r], update_recv.at[row], UPDATE, (col, r)))
+    update_recv[row] = update_send[row]
+
+    wait_for(score_recv.at[pl.ds(0, count - 1)], recv_sem, SCORE_GRAD)
+    bias_grad = jnp.sum(score_recv[...], axis=0)
+    picked = jnp.where(own_lane, bias_grad[:, None, :], 0.0).reshape(rows * cols, heads * tokens)
+    bias_sums = dot(picked, block_scaled, 0, 0).reshape(heads, tokens, width)
+    small_send[0:heads, :] = jnp.sum(bias_sums, axis=1)
+    small_send[heads : heads + 1, :] = jnp.sum(d_gate, axis=0, keepdims=True)
+    small_send[heads + 1 : heads + 2, :] = jnp.sum(d_normed * scaled, axis=0, keepdims=True)
+    to_all(lambda d: remote(small_send, small_recv.at[me], SMALL, device(d)))
+    small_recv[me] = small_send[...]
+    bias_part = layer_norm_back(dot(picked, spread_bias) * gain, block_scaled, block_inverse).reshape(
+        rows, cols, width
+    )
+
+    share_scale = 1.0 / tokens
+    for which in range(2):
+        first, number = CORE_SETS[which]
+
+        @pl.when(core == which)
+        def _(first=first, number=number):
+            mine = pl.ds(pl.multiple_of(chip * tile, tile), tile)
+            wait_for(scatter_recv.at[pl.ds(0, chips - 1), pl.ds(0, number)], recv_sem, SCATTER)
+            scatter_recv[chip, pl.ds(0, number)] = parts[pl.ds(first, number), mine, :]
+            total = jnp.sum(scatter_recv[:, pl.ds(0, number)], axis=0) * share_scale
+            gather_send[pl.ds(0, number)] = total
+            final[pl.ds(first, number), mine, :] = total
+
+            def step(distance, carry):
+                target = lax.rem(chip + distance, chips)
+                remote(
+                    gather_send.at[pl.ds(0, number)],
+                    final.at[pl.ds(first, number), mine, :],
+                    GATHER,
+                    (lax.rem(target, half_cols) * 2 + core, target // half_cols),
+                ).start()
+                return carry
+
+            lax.fori_loop(1, chips, step, 0)
+
+    wait_for(grad_recv.at[pl.ds(0, row_count - 1)], recv_sem, CELL_GRAD)
+    wait_for(update_recv.at[pl.ds(0, row_count - 1)], recv_sem, UPDATE)
+    for slot in range(cols):
+        pair_out[:, slot, :] = grad_recv[slot] + bias_part[:, slot, :]
+        update_out[:, slot, :] = update_recv[slot]
+    wait_for(small_recv.at[pl.ds(0, count - 1)], recv_sem, SMALL)
+    small = jnp.sum(small_recv[...], axis=0) * share_scale
+    bias_out[...] = small[:heads] * gain
+    gate_bias_out[...] = small[heads : heads + 1]
+    gain_out[...] = small[heads + 1 : heads + 2] + jnp.sum(
+        small[:heads] * wb_ref[...], axis=0, keepdims=True
+    )
+
+    for which in range(2):
+        first, number = CORE_SETS[which]
+        other_first, other_number = CORE_SETS[1 - which]
+
+        @pl.when(core == which)
+        def _(first=first, number=number, other_first=other_first, other_number=other_number):
+            some = scatter_recv.at[pl.ds(0, chips - 1), pl.ds(0, number)]
+            wait_for(some, recv_sem, GATHER)
+            forward = final.at[pl.ds(first, number)]
+            remote(forward, forward, FORWARD, partner).start()
+            wait_for(final.at[pl.ds(other_first, other_number)], recv_sem, FORWARD)
+            wait_for(some, send_sem, SCATTER)
+            wait_for(some, send_sem, GATHER)
+            wait_for(forward, send_sem, FORWARD)
+            for index in range(other_first, other_first + other_number):
+                wait_for(parts.at[index], send_sem, PAIR + index)
+
+    wo_out[...] = final[0]
+    gate_out[...] = final[1]
+    value_out[...] = final[2]
+    query_out[...] = final[3]
+    key_out[...] = final[4]
+    wait_for(cell_recv.at[pl.ds(0, row_count - 1)], send_sem, CELLS)
+    wait_for(bias_recv.at[pl.ds(0, count - 1)], send_sem, BIAS)
+    wait_for(update_recv.at[pl.ds(0, row_count - 1)], send_sem, UPDATE)
+    wait_for(grad_recv.at[pl.ds(0, row_count - 1)], send_sem, CELL_GRAD)
+    wait_for(score_recv.at[pl.ds(0, count - 1)], send_sem, SCORE_GRAD)
+    wait_for(small_recv.at[pl.ds(0, count - 1)], send_sem, SMALL)
+
+
+def body_fused(
+    row_count, col_count, tokens,
+    pair_rep, cotangent, chain_ids, template, norm_gain,
+    w_query, w_key, w_value, w_gate, gate_bias, w_out, w_bias,
+):
+    rows, cols, width = pair_rep.shape
+    heads = w_bias.shape[0]
+    count = row_count * col_count
+    chips = count // 2
+    tile = width // chips
+    number = CORE_SETS[0][1]
+    f32 = jnp.float32
+
+    def shape(*dims):
+        return jax.ShapeDtypeStruct(dims, f32)
+
+    def vmem(*dims):
+        return pltpu.VMEM(dims, f32)
+
+    square = shape(width, width)
+    out = pl.pallas_call(
+        functools.partial(fused_kernel, row_count, col_count, tokens, heads, template.shape[0]),
+        out_shape=(
+            shape(rows, cols, width), shape(rows, cols, width), square, square, square, square,
+            shape(1, width), square, shape(heads, width), shape(1, width),
+        ),
+        in_specs=[pl.BlockSpec(memory_space=pltpu.VMEM)] * 12,
+        out_specs=[pl.BlockSpec(memory_space=pltpu.VMEM)] * 10,
+        scratch_shapes=[
+            vmem(cols, 2 * rows, width), vmem(row_count, 2 * rows, width),
+            vmem(rows, width), vmem(count, rows, width), vmem(tokens, width),
+            vmem(row_count, rows, width), vmem(row_count, rows, width),
+            vmem(row_count, rows, width), vmem(row_count, rows, width),
+            vmem(row_count, rows, width), vmem(count, rows, width),
+            vmem(heads + 2, width), vmem(count, heads + 2, width),
+            vmem(MATRICES, width, width), vmem(MATRICES, width, width),
+            vmem(chips, number, tile, width), vmem(number, tile, width), vmem(MATRICES, width, width),
+            pltpu.SemaphoreType.DMA((PAIR + MATRICES,)),
+            pltpu.SemaphoreType.DMA((PAIR + MATRICES,)),
+        ],
+        compiler_params=pltpu.CompilerParams(
+            collective_id=0, has_side_effects=True, vmem_limit_bytes=32 * 1024 * 1024
+        ),
+        name="triangle",
+    )(
+        pair_rep, cotangent, chain_ids.reshape(1, -1), template, norm_gain.reshape(1, -1),
+        w_query, w_key, w_value, w_gate, gate_bias.reshape(1, -1), w_out, w_bias,
+    )
+    return out[:6] + (out[6].reshape(width),) + out[7:9] + (out[9].reshape(width),)
+
+
+def body(*arrays):
+    row_count, col_count = lax.axis_size("row"), lax.axis_size("col")
+    rows, cols, width = arrays[0].shape
+    tokens = rows * row_count
+    heads = arrays[11].shape[0]
+    chips = row_count * col_count // 2
+    fits = heads * tokens == LANES and width == LANES and width % (chips * SUBLANES) == 0
+    if fits and cols == row_count and col_count % 2 == 0:
+        return body_fused(row_count, col_count, tokens, *arrays)
+    return body_collective(*arrays)
+
+
 def solution(mesh):
     in_specs = (
         P("row", "col", None),

time: 332 us -> 41.8 us (0.13)
  blocking collectives: 149 us -> 0 us
  waiting for transfers between devices: 122 us -> 0 us
  Pallas kernels: 0 us -> 27.7 us
  starting transfers between devices: 20.2 us -> 0 us
  between operations: 14.3 us -> 0.7 us
  matrix products: 10.4 us -> 0 us
  other arithmetic: 5.79 us -> 0 us
  local copies, waits for them, and re-layouts: 8.98 us -> 12.9 us
    psum x1 -> x0, waiting for transfers between devices: 115 us -> none  [body(): lax.psum((grad_query_w, grad_key_w, grad_value_w, grad_gate_w, grad_gate_...]
    all_gather x1 -> x0, blocking collectives: 67.6 us -> none  [body(): bias_rows = lax.all_gather(bias_piece, ('col', 'row'), axis=0, tiled=True)]
    psum x1 -> x0, blocking collectives: 41 us -> none  [body(): lax.psum((grad_query_w, grad_key_w, grad_value_w, grad_gate_w, grad_gate_...]
    unnamed x1 -> x0, blocking collectives: 40 us -> none
    pallas_call x0 -> x1, Pallas kernels: none -> 27.7 us  [body_fused(): pl.pallas_call(functools.partial(fused_kernel, row_count, col_count, toke...]
    all_to_all x4 -> x0, starting transfers between devices: 20.1 us -> none  [the longest x1 7.38 us: body(): lax.all_to_all(pair_rep, 'row', split_axis=1, concat_axis=0, tiled=True)]
    dot_general x24 -> x0, matrix products: 10.4 us -> none  [the longest x15 8.05 us: matmul(): jnp.dot(left, right, precision=HIGHEST, preferred_element_type=jnp.float32)]
    all_to_all x4 -> x0, waiting for transfers between devices: 7.41 us -> none  [the longest x1 5.47 us: body(): lax.all_to_all(d_input.reshape(tokens, cols, width), 'row', split_axis=0,...]
  transfers between devices with their start and end apart: 5 -> 0, of which waited for: 3 -> 0; matrix products, arithmetic and copies ran while one was open for 4% -> 0% of each run, Pallas kernels for 0% -> 0%
where the time goes in v1:
time: 41.8 us; the launch traced here: 41.3 us
  Pallas kernels  27.7 us (66%)
  local copies, waits for them, and re-layouts  12.9 us (31%)
  between operations  0.7 us (2%)
    pallas_call x1, Pallas kernels, body_fused(): pl.pallas_call(functools.partial(fused_kernel, row_count, col_count, toke...  27.7 us
    unnamed x34, local copies, waits for them, and re-layouts  12.9 us

profile of v1, /device:TPU:0, one launch (start us, length us, event | category | flops | bytes accessed | tf_op | source)
XLA Modules:
  0.0 41.3 jit_solution(4194349023666295350)
XLA Ops:
  0.6 0.0 copy-start.7
  0.7 0.0 copy-start.9
  0.7 0.0 copy-start.10
  0.7 0.0 copy-start.11
  0.7 0.6 %copy-done.7 = s32[8,8]{1,0:T(8,128)S(1)} copy-done((s32[8,8]{1,0:T(8,128)S(1)}, s32[8,8]{1,0:T(8,128)}, u32[]{:S(2)}) %copy-start.7) | copy-done | bytes 280
  1.3 0.0 copy-done.9
  1.3 0.0 copy-done.10
  1.3 0.0 copy-done.11
  1.4 0.0 copy-start
  1.4 0.8 %copy-done = f32[128,128]{1,0:T(8,128)S(1)} copy-done((f32[128,128]{1,0:T(8,128)S(1)}, f32[128,128]{1,0:T(8,128)}, u32[]{:S(2)}) %copy-start) | copy-done | bytes 65560
  2.2 0.0 copy-start.1
  2.2 0.8 %copy-done.1 = f32[128,128]{1,0:T(8,128)S(1)} copy-done((f32[128,128]{1,0:T(8,128)S(1)}, f32[128,128]{1,0:T(8,128)}, u32[]{:S(2)}) %copy-start.1) | copy-done | bytes 65560
  3.0 0.0 copy-start.2
  3.0 0.8 %copy-done.2 = f32[128,128]{1,0:T(8,128)S(1)} copy-done((f32[128,128]{1,0:T(8,128)S(1)}, f32[128,128]{1,0:T(8,128)}, u32[]{:S(2)}) %copy-start.2) | copy-done | bytes 65560
  3.9 0.0 copy-start.3
  3.9 0.8 %copy-done.3 = f32[128,128]{1,0:T(8,128)S(1)} copy-done((f32[128,128]{1,0:T(8,128)S(1)}, f32[128,128]{1,0:T(8,128)}, u32[]{:S(2)}) %copy-start.3) | copy-done | bytes 65560
  4.7 0.0 copy-start.4
  4.7 0.8 %copy-done.4 = f32[128,128]{1,0:T(8,128)S(1)} copy-done((f32[128,128]{1,0:T(8,128)S(1)}, f32[128,128]{1,0:T(8,128)}, u32[]{:S(2)}) %copy-start.4) | copy-done | bytes 65560
  5.6 0.7 %copy-done.5 = f32[4,8,128]{2,1,0:T(8,128)S(1)} copy-done((f32[4,8,128]{2,1,0:T(8,128)S(1)}, f32[4,8,128]{2,1,0:T(8,128)}, u32[]{:S(2)}) %copy-start.5) | copy-done | bytes 16408
  6.3 0.7 %copy-done.6 = f32[4,8,128]{2,1,0:T(8,128)S(1)} copy-done((f32[4,8,128]{2,1,0:T(8,128)S(1)}, f32[4,8,128]{2,1,0:T(8,128)}, u32[]{:S(2)}) %copy-start.6) | copy-done | bytes 16408
  7.0 0.7 %copy-done.8 = f32[4,128]{1,0:T(4,128)S(1)} copy-done((f32[4,128]{1,0:T(4,128)S(1)}, f32[4,128]{1,0:T(4,128)}, u32[]{:S(2)}) %copy-start.8) | copy-done | bytes 2072
  7.7 27.7 %triangle.1 = (f32[4,8,128]{2,1,0:T(8,128)S(1)}, f32[4,8,128]{2,1,0:T(8,128)S(1)}, f32[128,128]{1,0:T(8,128)S(1)}, f32[128,128]{1,0:T(8,128)S(1)}, f32[128,128]{...) custom-call(f32[4,8,128]{2,1,0:T(8,128)S(1)} %copy-done.5, ...), custom_call_target="tpu_custom_call" | custom-call | tf_op jit(solution)/shard_map/triangle/pallas_call | solution.py:500
  35.3 0.6 %copy.32 = f32[4,8,128]{2,1,0:T(8,128)} copy(f32[4,8,128]{2,1,0:T(8,128)S(1)} %get-tuple-element.40) | data formatting | bytes 32768
  36.0 0.6 %copy.33 = f32[4,8,128]{2,1,0:T(8,128)} copy(f32[4,8,128]{2,1,0:T(8,128)S(1)} %get-tuple-element.41) | data formatting | bytes 32768
  36.6 0.6 %copy.34 = f32[128,128]{1,0:T(8,128)} copy(f32[128,128]{1,0:T(8,128)S(1)} %get-tuple-element.42) | data formatting | bytes 131072
  37.2 0.6 %copy.35 = f32[128,128]{1,0:T(8,128)} copy(f32[128,128]{1,0:T(8,128)S(1)} %get-tuple-element.43) | data formatting | bytes 131072
  37.8 0.6 %copy.36 = f32[128,128]{1,0:T(8,128)} copy(f32[128,128]{1,0:T(8,128)S(1)} %get-tuple-element.44) | data formatting | bytes 131072
  38.4 0.6 %copy.37 = f32[128,128]{1,0:T(8,128)} copy(f32[128,128]{1,0:T(8,128)S(1)} %get-tuple-element.45) | data formatting | bytes 131072
  39.1 0.5 %copy.38 = f32[128]{0:T(128)} copy(f32[128]{0:T(128)S(1)} %bitcast.9) | data formatting | bytes 1024
  39.6 0.6 %copy.39 = f32[128,128]{1,0:T(8,128)} copy(f32[128,128]{1,0:T(8,128)S(1)} %get-tuple-element.47) | data formatting | bytes 131072
  40.2 0.6 %copy.40 = f32[4,128]{1,0:T(4,128)} copy(f32[4,128]{1,0:T(4,128)S(1)} %get-tuple-element.48) | data formatting | bytes 4096
  40.8 0.5 %copy.41 = f32[128]{0:T(128)} copy(f32[128]{0:T(128)S(1)} %bitcast.8) | data formatting | bytes 1024
  (3 shorter events, 0.0 us)
Async XLA Ops:
  0.6 0.7 %copy-start.7 = (s32[8,8]{1,0:T(8,128)S(1)}, s32[8,8]{1,0:T(8,128)}, u32[]{:S(2)}) copy-start(s32[8,8]{1,0:T(8,128)} %template_ref.1) | copy-start | bytes 772
  0.7 0.7 %copy-start.9 = (s32[32]{0:T(128)S(1)}, s32[32]{0:T(128)}, u32[]{:S(2)}) copy-start(s32[32]{0:T(128)} %param.14) | copy-start | bytes 388
  0.7 0.7 %copy-start.10 = (f32[128]{0:T(128)S(1)}, f32[128]{0:T(128)}, u32[]{:S(2)}) copy-start(f32[128]{0:T(128)} %param.16) | copy-start | bytes 1540
  0.7 0.7 %copy-start.11 = (f32[128]{0:T(128)S(1)}, f32[128]{0:T(128)}, u32[]{:S(2)}) copy-start(f32[128]{0:T(128)} %param.21) | copy-start | bytes 1540
  1.4 0.8 %copy-start = (f32[128,128]{1,0:T(8,128)S(1)}, f32[128,128]{1,0:T(8,128)}, u32[]{:S(2)}) copy-start(f32[128,128]{1,0:T(8,128)} %wq_ref.1) | copy-start | bytes 196612
  2.2 0.8 %copy-start.1 = (f32[128,128]{1,0:T(8,128)S(1)}, f32[128,128]{1,0:T(8,128)}, u32[]{:S(2)}) copy-start(f32[128,128]{1,0:T(8,128)} %wk_ref.1) | copy-start | bytes 196612
  3.0 0.8 %copy-start.2 = (f32[128,128]{1,0:T(8,128)S(1)}, f32[128,128]{1,0:T(8,128)}, u32[]{:S(2)}) copy-start(f32[128,128]{1,0:T(8,128)} %wv_ref.1) | copy-start | bytes 196612
  3.9 0.8 %copy-start.3 = (f32[128,128]{1,0:T(8,128)S(1)}, f32[128,128]{1,0:T(8,128)}, u32[]{:S(2)}) copy-start(f32[128,128]{1,0:T(8,128)} %wg_ref.1) | copy-start | bytes 196612
  4.7 0.8 %copy-start.4 = (f32[128,128]{1,0:T(8,128)S(1)}, f32[128,128]{1,0:T(8,128)}, u32[]{:S(2)}) copy-start(f32[128,128]{1,0:T(8,128)} %wo_ref.1) | copy-start | bytes 196612
  5.6 0.7 %copy-start.5 = (f32[4,8,128]{2,1,0:T(8,128)S(1)}, f32[4,8,128]{2,1,0:T(8,128)}, u32[]{:S(2)}) copy-start(f32[4,8,128]{2,1,0:T(8,128)} %pair_ref.1) | copy-start | bytes 49156
  6.3 0.7 %copy-start.6 = (f32[4,8,128]{2,1,0:T(8,128)S(1)}, f32[4,8,128]{2,1,0:T(8,128)}, u32[]{:S(2)}) copy-start(f32[4,8,128]{2,1,0:T(8,128)} %cot_ref.1) | copy-start | bytes 49156
  7.0 0.7 %copy-start.8 = (f32[4,128]{1,0:T(4,128)S(1)}, f32[4,128]{1,0:T(4,128)}, u32[]{:S(2)}) copy-start(f32[4,128]{1,0:T(4,128)} %wb_ref.1) | copy-start | bytes 6148

commit v2 on v1

--- a/solution.py
+++ b/solution.py
@@ -203,13 +203,35 @@
 
 def fused_kernel(
     row_count, col_count, tokens, heads, blocks,
+    pair_in, cot_in, chain_in, template_in, gain_in,
+    wq_in, wk_in, wv_in, wg_in, gate_bias_in, wo_in, wb_in,
+    update_hbm, pair_hbm, query_hbm, key_hbm, value_hbm, gate_hbm, gate_bias_hbm, wo_hbm, bias_hbm, gain_hbm,
+    cell_send, cell_recv, bias_send, bias_recv, bias_full, update_send, update_recv,
+    grad_send, grad_recv, score_send, score_recv, small_send, small_recv,
+    parts, pair_recv, scatter_recv, gather_send, final,
     pair_ref, cot_ref, chain_ref, template_ref, gain_ref,
     wq_ref, wk_ref, wv_ref, wg_ref, gate_bias_ref, wo_ref, wb_ref,
-    update_out, pair_out, query_out, key_out, value_out, gate_out, gate_bias_out, wo_out, bias_out, gain_out,
-    cell_send, cell_recv, bias_send, bias_recv, bias_full, update_send, update_recv,
-    grad_send, grad_recv, score_send, score_recv, small_send, small_recv,
-    parts, pair_recv, scatter_recv, gather_send, final, send_sem, recv_sem,
+    update_out, pair_out, bias_out, gate_bias_out, gain_out,
+    send_sem, recv_sem, load_sem, store_sem,
 ):
+    loads = [
+        pltpu.make_async_copy(source, held, load_sem.at[index])
+        for index, (source, held) in enumerate(
+            (
+                (pair_in, pair_ref), (cot_in, cot_ref), (gain_in, gain_ref), (wb_in, wb_ref),
+                (chain_in, chain_ref), (template_in, template_ref), (wq_in, wq_ref), (wk_in, wk_ref),
+                (wv_in, wv_ref), (wg_in, wg_ref), (gate_bias_in, gate_bias_ref), (wo_in, wo_ref),
+            )
+        )
+    ]
+    for load in loads:
+        load.start()
+    stores = []
+
+    def store(held, target):
+        copy = pltpu.make_async_copy(held, target, store_sem.at[len(stores)])
+        copy.start()
+        stores.append(copy)
     width = LANES
     depth = width // heads
     factor = depth ** (-0.5)
@@ -260,6 +282,8 @@
 
     lax.fori_loop(1, count, greet, 0)
 
+    for load in loads[:4]:
+        load.wait()
     for slot in range(cols):
         cell_send[slot, :rows, :] = pair_ref[:, slot, :]
         cell_send[slot, rows:, :] = cot_ref[:, slot, :]
@@ -280,6 +304,8 @@
     cell_recv[row] = cell_send[row]
     bias_recv[me] = bias_send[...]
 
+    for load in loads[4:]:
+        load.wait()
     own = col * cols + row
     token_shift = (tokens // blocks).bit_length() - 1
     chain_row = chain_ref[...].astype(jnp.float32)
@@ -439,6 +465,8 @@
     for slot in range(cols):
         pair_out[:, slot, :] = grad_recv[slot] + bias_part[:, slot, :]
         update_out[:, slot, :] = update_recv[slot]
+    store(pair_out, pair_hbm)
+    store(update_out, update_hbm)
     wait_for(small_recv.at[pl.ds(0, count - 1)], recv_sem, SMALL)
     small = jnp.sum(small_recv[...], axis=0) * share_scale
     bias_out[...] = small[:heads] * gain
@@ -446,6 +474,9 @@
     gain_out[...] = small[heads + 1 : heads + 2] + jnp.sum(
         small[:heads] * wb_ref[...], axis=0, keepdims=True
     )
+    store(bias_out, bias_hbm)
+    store(gate_bias_out, gate_bias_hbm)
+    store(gain_out, gain_hbm)
 
     for which in range(2):
         first, number = CORE_SETS[which]
@@ -464,17 +495,26 @@
             for index in range(other_first, other_first + other_number):
                 wait_for(parts.at[index], send_sem, PAIR + index)
 
-    wo_out[...] = final[0]
-    gate_out[...] = final[1]
-    value_out[...] = final[2]
-    query_out[...] = final[3]
-    key_out[...] = final[4]
+    for index, target in enumerate((wo_hbm, gate_hbm, value_hbm, query_hbm, key_hbm)):
+        store(final.at[index], target)
     wait_for(cell_recv.at[pl.ds(0, row_count - 1)], send_sem, CELLS)
     wait_for(bias_recv.at[pl.ds(0, count - 1)], send_sem, BIAS)
     wait_for(update_recv.at[pl.ds(0, row_count - 1)], send_sem, UPDATE)
     wait_for(grad_recv.at[pl.ds(0, row_count - 1)], send_sem, CELL_GRAD)
     wait_for(score_recv.at[pl.ds(0, count - 1)], send_sem, SCORE_GRAD)
     wait_for(small_recv.at[pl.ds(0, count - 1)], send_sem, SMALL)
+    for copy in stores:
+        copy.wait()
+
+
+def store_kernel(*refs):
+    copies = [
+        pltpu.make_async_copy(refs[index], refs[10 + index], refs[20].at[index]) for index in range(10)
+    ]
+    for copy in copies:
+        copy.start()
+    for copy in copies:
+        copy.wait()
 
 
 def body_fused(
@@ -489,6 +529,10 @@
     tile = width // chips
     number = CORE_SETS[0][1]
     f32 = jnp.float32
+    arrays = (
+        pair_rep, cotangent, chain_ids.reshape(1, -1), template, norm_gain.reshape(1, -1),
+        w_query, w_key, w_value, w_gate, gate_bias.reshape(1, -1), w_out, w_bias,
+    )
 
     def shape(*dims):
         return jax.ShapeDtypeStruct(dims, f32)
@@ -503,8 +547,8 @@
             shape(rows, cols, width), shape(rows, cols, width), square, square, square, square,
             shape(1, width), square, shape(heads, width), shape(1, width),
         ),
-        in_specs=[pl.BlockSpec(memory_space=pltpu.VMEM)] * 12,
-        out_specs=[pl.BlockSpec(memory_space=pltpu.VMEM)] * 10,
+        in_specs=[pl.BlockSpec(memory_space=pltpu.HBM)] * 12,
+        out_specs=[pl.BlockSpec(memory_space=pltpu.HBM)] * 10,
         scratch_shapes=[
             vmem(cols, 2 * rows, width), vmem(row_count, 2 * rows, width),
             vmem(rows, width), vmem(count, rows, width), vmem(tokens, width),
@@ -514,18 +558,29 @@
             vmem(heads + 2, width), vmem(count, heads + 2, width),
             vmem(MATRICES, width, width), vmem(MATRICES, width, width),
             vmem(chips, number, tile, width), vmem(number, tile, width), vmem(MATRICES, width, width),
+            *[pltpu.VMEM(array.shape, array.dtype) for array in arrays],
+            vmem(rows, cols, width), vmem(rows, cols, width),
+            vmem(heads, width), vmem(1, width), vmem(1, width),
             pltpu.SemaphoreType.DMA((PAIR + MATRICES,)),
             pltpu.SemaphoreType.DMA((PAIR + MATRICES,)),
+            pltpu.SemaphoreType.DMA((len(arrays),)),
+            pltpu.SemaphoreType.DMA((10,)),
         ],
         compiler_params=pltpu.CompilerParams(
-            collective_id=0, has_side_effects=True, vmem_limit_bytes=32 * 1024 * 1024
+            collective_id=0, has_side_effects=True, vmem_limit_bytes=63 * 1024 * 1024
         ),
         name="triangle",
-    )(
-        pair_rep, cotangent, chain_ids.reshape(1, -1), template, norm_gain.reshape(1, -1),
-        w_query, w_key, w_value, w_gate, gate_bias.reshape(1, -1), w_out, w_bias,
-    )
-    return out[:6] + (out[6].reshape(width),) + out[7:9] + (out[9].reshape(width),)
+    )(*arrays)
+    out = pl.pallas_call(
+        store_kernel,
+        out_shape=[jax.ShapeDtypeStruct(array.shape, array.dtype) for array in out],
+        in_specs=[pl.BlockSpec(memory_space=pltpu.HBM)] * 10,
+        out_specs=[pl.BlockSpec(memory_space=pltpu.HBM)] * 10,
+        scratch_shapes=[pltpu.SemaphoreType.DMA((10,))],
+        compiler_params=pltpu.CompilerParams(vmem_limit_bytes=63 * 1024 * 1024),
+        name="store",
+    )(*out)
+    return tuple(out[:6]) + (out[6].reshape(width),) + tuple(out[7:9]) + (out[9].reshape(width),)
 
 
 def body(*arrays):

time: 41.8 us -> 41.4 us (level)
  local copies, waits for them, and re-layouts: 12.9 us -> 0 us
  Pallas kernels: 27.7 us -> 40.5 us
    unnamed x34 -> x0, local copies, waits for them, and re-layouts: 12.9 us -> none
    pallas_call x0 -> x1, Pallas kernels: none -> 12.2 us  [body_fused(): pl.pallas_call(store_kernel, out_shape=[jax.ShapeDtypeStruct(array.shape,...]
    pallas_call x1, Pallas kernels: 27.7 us -> 28.3 us  [body_fused(): pl.pallas_call(functools.partial(fused_kernel, row_count, col_count, toke...]
where the time goes in v2:
time: 41.4 us; the launch traced here: 41.2 us
  Pallas kernels  40.5 us (98%)
  between operations  0.66 us (2%)
    pallas_call x1, Pallas kernels, body_fused(): pl.pallas_call(functools.partial(fused_kernel, row_count, col_count, toke...  28.3 us
    pallas_call x1, Pallas kernels, body_fused(): pl.pallas_call(store_kernel, out_shape=[jax.ShapeDtypeStruct(array.shape,...  12.2 us

profile of v2, /device:TPU:0, one launch (start us, length us, event | category | flops | bytes accessed | tf_op | source)
XLA Modules:
  0.0 41.2 jit_solution(17924269378400213755)
XLA Ops:
  0.6 28.3 %triangle.1 = (f32[4,8,128]{2,1,0:T(8,128)}, f32[4,8,128]{2,1,0:T(8,128)}, f32[128,128]{1,0:T(8,128)}, f32[128,128]{1,0:T(8,128)}, f32[128,128]{1,0:T(8,128)}, /...) custom-call(f32[4,8,128]{2,1,0:T(8,128)} %pair_in.1, ...), custom_call_target="tpu_custom_call" | custom-call | tf_op jit(solution)/shard_map/triangle/pallas_call | solution.py:544
  29.0 12.2 %store.1 = (f32[4,8,128]{2,1,0:T(8,128)}, f32[4,8,128]{2,1,0:T(8,128)}, f32[128,128]{1,0:T(8,128)}, f32[128,128]{1,0:T(8,128)}, f32[128,128]{1,0:T(8,128)}, /*in...) custom-call(f32[4,8,128]{2,1,0:T(8,128)} %get-tuple-element.30.refs_0_, ...), custom_call_target="tpu_custom_call" | custom-call | tf_op jit(solution)/shard_map/store/pallas_call | solution.py:574
